TPU v7x, 32 devices: a whole 2x2x4 slice. The times are simulated.
32 devices in a mesh: row: 4 (over y, x), col: 8 (over z, core).
Axes of the slice: x: 2, y: 2, z: 4, core: 2. Of those that a mesh axis runs over, the one named last changes fastest.
Arguments:
- g_first: float32 [1024, 2048], P('col'), may hold values from -6 to 6
- g_second: float32 [1024, 2048], P('col'), may hold values from -6 to 6
- y_head: float32 [63488, 2048], P(('row', 'col')), may hold values from -6 to 6
- l_rows: float32 [2048, 63488], P(None, ('row', 'col')), may hold values from -0.125 to 0.125
- ut_first_inv: float32 [1024, 1024], P('row', 'col'), as said below
- ut_cross: float32 [1024, 1024], P('col', 'row'), may hold values from -0.09375 to 0.09375
- ut_second_inv: float32 [1024, 1024], P('row', 'col'), as said below
- lt_second_inv: float32 [1024, 1024], P('col', 'row'), as said below
- lt_cross: float32 [1024, 1024], P('row', 'col'), may hold values from -0.09375 to 0.09375
- lt_first_inv: float32 [1024, 1024], P('col', 'row'), as said below
Outputs:
- x_first: float32 [1024, 2048], P('col', 'row')
- x_second: float32 [1024, 2048], P('col', 'row')
- head_out: float32 [63488, 2048], P(('row', 'col'))
Inputs may be any that keep to these rules, and one draw needn't show every extreme that they name: `ut_first_inv`: lower triangular with a positive diagonal. `ut_second_inv`: lower triangular with a positive diagonal. `lt_second_inv`: upper triangular with a unit diagonal. `lt_first_inv`: upper triangular with a unit diagonal.
All inputs are finite; a program needn't handle non-finite values.
Results may differ from a plain program's by a relative error of at most 0.000084.
Values sent between devices are 32-bit elements; how exact they have to be, the bound alone decides.
A program may use at most 192 MiB of HBM per device.

v0:
```python
import jax
import jax.numpy as jnp
from jax import lax
from jax.sharding import PartitionSpec as P


def product(left, right):
    return jnp.dot(left, right, precision=lax.Precision.HIGHEST, preferred_element_type=jnp.float32)


def transposed_product(rows_block, vector):
    return lax.dot_general(
        rows_block,
        vector,
        (((0,), (0,)), ((), ())),
        precision=lax.Precision.HIGHEST,
        preferred_element_type=jnp.float32,
    )


def apply_over_col(matrix, vector):
    return lax.psum(product(matrix, vector), "col")


def apply_over_row(matrix, vector):
    return lax.psum(product(matrix, vector), "row")


def shards(
    g_first,
    g_second,
    y_head,
    l_rows,
    ut_first_inv,
    ut_cross,
    ut_second_inv,
    lt_second_inv,
    lt_cross,
    lt_first_inv,
):
    panel = l_rows.shape[0] // 2
    initial = jnp.zeros(y_head.shape, jnp.float32)

    def fold_from(base, running, pieces):
        block = lax.dynamic_slice_in_dim(l_rows, base, pieces.shape[0], 0)
        return running + transposed_product(block, pieces)

    y_first = apply_over_col(ut_first_inv, g_first)
    shifted = g_second - apply_over_row(ut_cross, y_first)
    y_second = apply_over_col(ut_second_inv, shifted)
    x_second = apply_over_row(lt_second_inv, y_second)
    corrected = y_first - apply_over_col(lt_cross, x_second)
    x_first = apply_over_row(lt_first_inv, corrected)
    pieces = (
        lax.all_gather(x_first, "col", axis=0, tiled=True),
        lax.all_gather(x_second, "col", axis=0, tiled=True),
    )
    both_parts = fold_from(panel, fold_from(0, initial, pieces[0]), pieces[1])
    head_out = y_head - both_parts
    col_width = x_first.shape[1] // lax.axis_size("row")
    begin = lax.axis_index("row") * col_width
    first_block = lax.dynamic_slice_in_dim(x_first, begin, col_width, 1)
    second_block = lax.dynamic_slice_in_dim(x_second, begin, col_width, 1)
    return (first_block, second_block, head_out)


def solution(mesh):
    return jax.shard_map(
        shards,
        mesh=mesh,
        in_specs=(
            P("col", None),
            P("col", None),
            P(("row", "col"), None),
            P(None, ("row", "col")),
            P("row", "col"),
            P("col", "row"),
            P("row", "col"),
            P("col", "row"),
            P("row", "col"),
            P("col", "row"),
        ),
        out_specs=(P("col", "row"), P("col", "row"), P(("row", "col"), None)),
        check_vma=False,
    )
```

profile of v0, /device:TPU:0, one launch (start us, length us, event | category | flops | bytes accessed | tf_op | source)
XLA Modules:
  0.0 657.9 jit_solution(1066636074306241734)
XLA Ops:
  7.2 0.0 copy-start
  7.2 0.0 copy-start.3
  7.2 0.0 copy-start.4
  7.2 0.0 all-reduce.7.cloned.1.call-start
  7.2 1.1 copy-done
  8.4 4.0 fusion.8
  12.4 0.0 copy-start.5
  12.4 0.0 all-reduce.7.cloned.1.call-update
  12.5 0.0 all-reduce.9.cloned.1.call-start
  12.5 67.7 %all-reduce.7.cloned.1.call-done = f32[256,2048]{1,0:T(8,128)} async-done(((f32[256,2048]{1,0:T(8,128)}), f32[256,2048]{1,0:T(8,128)}) %all-reduce.7.cloned.1.call-update) | async-done | bytes 2097168 | tf_op jit(solution)/shard_map/psum | solution.py:22
  80.2 3.8 convolution_bitcast_fusion.4
  84.1 0.0 all-reduce.9.cloned.1.call-update
  84.1 0.0 copy-start.2
  84.1 0.0 copy-start.6
  84.1 0.0 all-reduce.11.cloned.1.call-start
  84.2 52.3 %all-reduce.9.cloned.1.call-done = f32[128,2048]{1,0:T(8,128)} async-done(((f32[128,2048]{1,0:T(8,128)}), f32[128,2048]{1,0:T(8,128)}) %all-reduce.9.cloned.1.call-update) | async-done | bytes 1048592 | tf_op jit(solution)/shard_map/psum | solution.py:26
  136.5 0.0 copy-done.3
  136.5 4.7 convolution_bitcast_fusion.1
  141.2 0.0 all-reduce.11.cloned.1.call-update
  141.2 0.0 all-reduce.13.cloned.1.call-start
  141.2 65.0 %all-reduce.11.cloned.1.call-done = f32[256,2048]{0,1:T(8,128)} async-done(((f32[256,2048]{0,1:T(8,128)}), f32[256,2048]{0,1:T(8,128)}) %all-reduce.11.cloned.1.call-update) | async-done | bytes 2097168 | tf_op jit(solution)/shard_map/psum | solution.py:22
  206.3 0.0 copy-done.4
  206.3 4.4 convolution_bitcast_fusion.3
  210.6 0.0 all-reduce.13.cloned.1.call-update
  210.7 0.0 all-reduce.15.cloned.1.call-start
  210.7 52.3 %all-reduce.13.cloned.1.call-done = f32[128,2048]{0,1:T(8,128)} async-done(((f32[128,2048]{0,1:T(8,128)}), f32[128,2048]{0,1:T(8,128)}) %all-reduce.13.cloned.1.call-update) | async-done | bytes 1048592 | tf_op jit(solution)/shard_map/psum | solution.py:26
  263.0 0.0 copy-done.5
  263.0 4.4 convolution_bitcast_fusion
  267.4 0.0 all-reduce.15.cloned.1.call-update
  267.4 0.2 all-reduce.17.cloned.1.call-start
  267.6 64.9 %all-reduce.15.cloned.1.call-done = f32[256,2048]{1,0:T(8,128)} async-done(((f32[256,2048]{1,0:T(8,128)}), f32[256,2048]{1,0:T(8,128)}) %all-reduce.15.cloned.1.call-update) | async-done | bytes 2097168 | tf_op jit(solution)/shard_map/psum | solution.py:22
  332.5 0.0 copy-done.2
  332.5 0.0 copy-done.6
  332.5 6.0 convolution_bitcast_fusion.2
  338.5 0.0 all-reduce.17.cloned.1.call-update
  338.5 0.0 all-gather.5.cloned.1.call-start
  338.6 0.7 all-gather.5.cloned.1.call-update
  339.3 0.0 all-gather.3.cloned.1.call-start
  339.3 51.6 %all-reduce.17.cloned.1.call-done = f32[128,2048]{0,1:T(8,128)} async-done(((f32[128,2048]{0,1:T(8,128)}), f32[128,2048]{0,1:T(8,128)}) %all-reduce.17.cloned.1.call-update) | async-done | bytes 1048592 | tf_op jit(solution)/shard_map/psum | solution.py:26
  390.9 0.0 all-gather.3.cloned.1.call-update
  390.9 1.0 constant_dynamic-slice_fusion
  391.9 0.8 copy.14
  392.7 1.0 constant_dynamic-slice_fusion.1
  393.7 0.8 copy.13
  394.5 80.5 %all-gather.5.cloned.1.call-done = f32[1024,2048]{0,1:T(8,128)} async-done(((f32[128,2048]{0,1:T(8,128)}), f32[1024,2048]{0,1:T(8,128)}) %all-gather.5.cloned.1.call-update) | async-done | bytes 8388624 | tf_op jit(solution)/shard_map/all_gather | solution.py:56
  475.0 57.2 %fusion = f32[2048,1984]{0,1:T(8,128)} fusion(f32[1024,2048]{0,1:T(8,128)} %all-gather.5.cloned.1.call-done, f32[2048,1984]{0,1:T(8,128)} %param.13), kind=kOutput, calls=%fused_computation.1 | convolution fusion | flops 49928994816 | bytes 32768000 | tf_op jit(solution)/shard_map/dot_general | solution.py:12
  532.2 25.1 %all-gather.3.cloned.1.call-done = f32[1024,2048]{0,1:T(8,128)} async-done(((f32[128,2048]{0,1:T(8,128)}), f32[1024,2048]{0,1:T(8,128)}) %all-gather.3.cloned.1.call-update) | async-done | bytes 8388624 | tf_op jit(solution)/shard_map/all_gather | solution.py:55
  557.3 0.0 copy-start.1
  557.3 93.7 %bitcast_subtract_fusion = f32[1984,2048]{1,0:T(8,128)} fusion(f32[1984,2048]{1,0:T(8,128)} %param.12, f32[2048,1984]{0,1:T(8,128)} %fusion, f32[1024,2048]{0,1:T(8,128)} %all-gather.3.cloned.1.call-done, f32[2048,1984]{0,1:T(8,128)} %param.13), kind=kOutput, calls=%fused_computation | convolution fusion | flops 49937121280 | bytes 65273856 | tf_op jit(solution)/shard_map/dot_general | solution.py:12
  651.0 0.0 copy-done.1
Async XLA Ops:
  7.2 1.2 copy-start
  7.2 129.3 %copy-start.3 = (f32[256,128]{1,0:T(8,128)S(1)}, f32[256,128]{1,0:T(8,128)}, u32[]{:S(2)}) copy-start(f32[256,128]{1,0:T(8,128)} %param.16) | copy-start | bytes 393220
  7.2 199.1 %copy-start.4 = (f32[128,256]{1,0:T(8,128)S(1)}, f32[128,256]{1,0:T(8,128)}, u32[]{:S(2)}) copy-start(f32[128,256]{1,0:T(8,128)} %param.17) | copy-start | bytes 393220
  7.2 73.0 %all-reduce.7.cloned.1.call-start = ((), (), s32[]{:S(2)}) async-start(), calls=%async_computation | async-start | bytes 4194304 | tf_op jit(solution)/shard_map/psum | solution.py:22
  12.4 250.6 %copy-start.5 = (f32[256,128]{1,0:T(8,128)S(1)}, f32[256,128]{1,0:T(8,128)}, u32[]{:S(2)}) copy-start(f32[256,128]{1,0:T(8,128)} %param.18) | copy-start | bytes 393220
  12.5 124.0 %all-reduce.9.cloned.1.call-start = ((), (), s32[]{:S(2)}) async-start(), calls=%async_computation.1 | async-start | bytes 2097152 | tf_op jit(solution)/shard_map/psum | solution.py:26
  84.1 248.4 %copy-start.2 = (f32[256,2048]{1,0:T(8,128)S(1)}, f32[256,2048]{1,0:T(8,128)}, u32[]{:S(2)}) copy-start(f32[256,2048]{1,0:T(8,128)} %all-reduce.7.cloned.1.call-done) | copy-start | bytes 6291460
  84.1 248.4 %copy-start.6 = (f32[128,256]{1,0:T(8,128)S(1)}, f32[128,256]{1,0:T(8,128)}, u32[]{:S(2)}) copy-start(f32[128,256]{1,0:T(8,128)} %param.19) | copy-start | bytes 393220
  84.1 122.1 %all-reduce.11.cloned.1.call-start = ((), (), s32[]{:S(2)}) async-start(), calls=%async_computation.2 | async-start | bytes 4194304 | tf_op jit(solution)/shard_map/psum | solution.py:22
  141.2 121.8 %all-reduce.13.cloned.1.call-start = ((), (), s32[]{:S(2)}) async-start(), calls=%async_computation.3 | async-start | bytes 2097152 | tf_op jit(solution)/shard_map/psum | solution.py:26
  210.7 121.8 %all-reduce.15.cloned.1.call-start = ((), (), s32[]{:S(2)}) async-start(), calls=%async_computation.4 | async-start | bytes 4194304 | tf_op jit(solution)/shard_map/psum | solution.py:22
  267.4 123.5 %all-reduce.17.cloned.1.call-start = ((), (), s32[]{:S(2)}) async-start(), calls=%async_computation.5 | async-start | bytes 2097152 | tf_op jit(solution)/shard_map/psum | solution.py:26
  338.5 136.5 %all-gather.5.cloned.1.call-start = ((), (), s32[]{:S(2)}) async-start(), calls=%async_computation.7 | async-start | bytes 9437184 | tf_op jit(solution)/shard_map/all_gather | solution.py:56
  339.3 218.0 %all-gather.3.cloned.1.call-start = ((), (), s32[]{:S(2)}) async-start(), calls=%async_computation.6 | async-start | bytes 9437184 | tf_op jit(solution)/shard_map/all_gather | solution.py:55
  557.3 93.7 %copy-start.1 = (f32[128,2048]{1,0:T(8,128)S(1)}, f32[128,2048]{1,0:T(8,128)}, u32[]{:S(2)}) copy-start(f32[128,2048]{1,0:T(8,128)} %param.10) | copy-start | bytes 3145732
Sparse Core Ops, SparseCore 0:
  12.6 67.6 all-reduce.6
  84.2 52.1 all-reduce.8
  141.3 64.9 all-reduce.10
  210.8 52.1 all-reduce.12
  267.5 64.9 all-reduce.14
  338.7 52.1 all-reduce.16
  392.5 82.4 all-gather.4
  476.6 80.6 all-gather.2
where the time goes:
time: 658 us
  waiting for transfers between devices  460 us (70%)
  matrix products  178 us (27%)
  between operations  14.2 us (2%)
    psum x3, waiting for transfers between devices, apply_over_col(): return lax.psum(product(matrix, vector), 'col')  198 us
    psum x3, waiting for transfers between devices, apply_over_row(): return lax.psum(product(matrix, vector), 'row')  156 us
    dot_general x2, matrix products, transposed_product(): lax.dot_general(rows_block, vector, (((0,), (0,)), ((), ())), precision=l...  151 us
    all_gather x1, waiting for transfers between devices, shards(): lax.all_gather(x_second, 'col', axis=0, tiled=True)  80.5 us
    dot_general x6, matrix products, product(): jnp.dot(left, right, precision=lax.Precision.HIGHEST, preferred_element_t...  27.3 us
    all_gather x1, waiting for transfers between devices, shards(): lax.all_gather(x_first, 'col', axis=0, tiled=True)  25.1 us
  transfers between devices with their start and end apart: 8, of which 8 were waited for; matrix products, arithmetic and copies ran while one was open for 9% of the time, Pallas kernels for 0%

commit v1 on v0

v1 whole, which is shorter than its diff:
```python
import jax
import jax.numpy as jnp
from jax import lax
from jax.sharding import PartitionSpec as P

BOTH = ("row", "col")


def times(left, right, left_dim, right_dim):
    return lax.dot_general(
        left,
        right,
        (((left_dim,), (right_dim,)), ((), ())),
        precision=lax.Precision.HIGH,
        preferred_element_type=jnp.float32,
    )


def shards(
    g_first,
    g_second,
    y_head,
    l_rows,
    ut_first_inv,
    ut_cross,
    ut_second_inv,
    lt_second_inv,
    lt_cross,
    lt_first_inv,
):
    panel = l_rows.shape[0] // 2
    rows, cols = lax.axis_size("row"), lax.axis_size("col")
    row, col = lax.axis_index("row"), lax.axis_index("col")
    width = g_first.shape[1] // rows
    depth = g_first.shape[0]

    def own_columns(g):
        return lax.dynamic_slice_in_dim(g, row * width, width, 1).T

    g = jnp.stack([own_columns(g_first), own_columns(g_second)], axis=1)
    g = lax.all_to_all(g, "col", 0, 2, tiled=True)

    def gather_pair(by_row, by_col):
        blocks = lax.all_gather(jnp.stack([by_row, by_col.T]), BOTH)
        tall, wide = by_row.shape
        blocks = blocks.reshape(rows, cols, 2, tall, wide).transpose(2, 0, 3, 1, 4)
        return blocks.reshape(2, panel, panel)

    first_pair = gather_pair(ut_first_inv, ut_cross)
    second_pair = gather_pair(ut_second_inv, lt_second_inv)
    third_pair = gather_pair(lt_cross, lt_first_inv)

    y_first = times(g[:, 0], first_pair[0], 1, 1)
    shifted = g[:, 1] - times(y_first, first_pair[1], 1, 0)
    y_second = times(shifted, second_pair[0], 1, 1)
    x_second = times(y_second, second_pair[1], 1, 0)
    second_all = lax.all_gather(x_second, BOTH, axis=0, tiled=True)
    corrected = y_first - times(x_second, third_pair[0], 1, 1)
    x_first = times(corrected, third_pair[1], 1, 0)
    first_all = lax.all_gather(x_first, BOTH, axis=0, tiled=True)

    head = y_head - times(l_rows[panel:], second_all, 0, 1)
    head = head - times(l_rows[:panel], first_all, 0, 1)

    def own_block(x):
        return lax.dynamic_slice(x, (row * width, col * depth), (width, depth)).T

    return (own_block(first_all), own_block(second_all), head)


def solution(mesh):
    return jax.shard_map(
        shards,
        mesh=mesh,
        in_specs=(
            P("col", None),
            P("col", None),
            P(("row", "col"), None),
            P(None, ("row", "col")),
            P("row", "col"),
            P("col", "row"),
            P("row", "col"),
            P("col", "row"),
            P("row", "col"),
            P("col", "row"),
        ),
        out_specs=(P("col", "row"), P("col", "row"), P(("row", "col"), None)),
        check_vma=False,
    )
```

time: 658 us -> 527 us (0.80); the launches traced: 658 us -> 517 us
  waiting for transfers between devices: 460 us -> 337 us
  matrix products: 178 us -> 85.5 us
  local copies, waits for them, and re-layouts: 4.8 us -> 48.8 us
  blocking collectives: 0 us -> 26.5 us
    psum x6 -> x0, waiting for transfers between devices: 354 us -> none  [the longest x3 198 us: apply_over_col(): return lax.psum(product(matrix, vector), 'col')]
    all_gather x2 -> x5, waiting for transfers between devices: 106 us -> 336 us  [the longest x3 183 us: gather_pair(): blocks = lax.all_gather(jnp.stack([by_row, by_col.T]), BOTH)]
    dot_general x8, matrix products: 178 us -> 85.5 us  [times(): lax.dot_general(left, right, (((left_dim,), (right_dim,)), ((), ())), pre...]
    reshape x0 -> x3, local copies, waits for them, and re-layouts: none -> 28.2 us  [gather_pair(): blocks = blocks.reshape(rows, cols, 2, tall, wide).transpose(2, 0, 3, 1, 4)]
    all_to_all x0 -> x1, blocking collectives: none -> 26.5 us  [shards(): g = lax.all_to_all(g, 'col', 0, 2, tiled=True)]
    slice x0 -> x3, local copies, waits for them, and re-layouts: none -> 12.5 us  [the longest x1 4.73 us: shards(): x_first = times(corrected, third_pair[1], 1, 0)]
  transfers between devices with their start and end apart: 8 -> 5, of which waited for: 8 -> 5; matrix products, arithmetic and copies ran while one was open for 9% -> 7% of each run, Pallas kernels for 0% -> 0%
where the time goes in v1:
time: 527 us; the launch traced here: 517 us
  waiting for transfers between devices  337 us (64%)
  matrix products  85.5 us (16%)
  local copies, waits for them, and re-layouts  48.8 us (9%)
  blocking collectives  26.5 us (5%)
  between operations  14.2 us (3%)
  other arithmetic  5.38 us (1%)
    all_gather x3, waiting for transfers between devices, gather_pair(): blocks = lax.all_gather(jnp.stack([by_row, by_col.T]), BOTH)  183 us
    dot_general x8, matrix products, times(): lax.dot_general(left, right, (((left_dim,), (right_dim,)), ((), ())), pre...  85.5 us
    all_gather x1, waiting for transfers between devices, shards(): second_all = lax.all_gather(x_second, BOTH, axis=0, tiled=True)  77.6 us
    all_gather x1, waiting for transfers between devices, shards(): first_all = lax.all_gather(x_first, BOTH, axis=0, tiled=True)  75.6 us
    reshape x3, local copies, waits for them, and re-layouts, gather_pair(): blocks = blocks.reshape(rows, cols, 2, tall, wide).transpose(2, 0, 3, 1, 4)  28.2 us
    all_to_all x1, blocking collectives, shards(): g = lax.all_to_all(g, 'col', 0, 2, tiled=True)  26.5 us
  transfers between devices with their start and end apart: 5, of which 5 were waited for; matrix products, arithmetic and copies ran while one was open for 7% of the time, Pallas kernels for 0%

profile of v1, /device:TPU:0, one launch (start us, length us, event | category | flops | bytes accessed | tf_op | source)
XLA Modules:
  0.0 517.3 jit_solution(12135769118998682857)
XLA Ops:
  7.2 0.0 all-gather.13.cloned.1.call-start
  7.2 1.0 copy.33
  8.2 1.6 pad_maximum_fusion.1
  9.8 0.0 all-gather.13.cloned.1.call-update
  9.9 0.0 all-gather.15.cloned.1.call-start
  9.9 1.0 copy.35
  10.9 1.6 pad_maximum_fusion.2
  12.5 0.0 all-gather.15.cloned.1.call-update
  12.6 0.0 all-gather.17.cloned.1.call-start
  12.6 1.0 copy.37
  13.6 1.6 pad_maximum_fusion.3
  15.3 0.0 all-gather.17.cloned.1.call-update
  15.3 0.0 all-gather.9.cloned.1.call-start
  15.3 1.1 constant_dynamic-slice_fusion
  16.4 0.1 copy.41
  16.5 0.1 copy.42
  16.7 0.5 pad_maximum_fusion
  17.2 26.5 %all_to_all.18 = f32[512,2,128]{2,1,0:T(2,128)S(1)} all-to-all(f32[512,2,128]{2,1,0:T(2,128)S(1)} %pad_maximum_fusion), channel_id=1, replica_groups=mesh['row'=4,'col'=8] {'col'}, dimensions={0} | all-to-all | bytes 1048576 | tf_op jit(solution)/shard_map/all_to_all | solution.py:41
  43.8 52.0 %all-gather.13.cloned.1.call-done = f32[64,256,128]{2,1,0:T(8,128)} async-done(((f32[2,256,128]{2,1,0:T(8,128)}), f32[64,256,128]{2,1,0:T(8,128)}) %all-gather.13.cloned.1.call-update) | async-done | bytes 8388624 | tf_op jit(solution)/shard_map/all_gather | solution.py:44
  95.8 11.5 %copy.84 = f32[4,8,2,256,128]{4,1,3,0,2:T(8,128)} copy(f32[4,8,2,256,128]{4,3,2,1,0:T(8,128)} %bitcast.104) | data formatting | bytes 16777216 | tf_op jit(solution)/shard_map/reshape | solution.py:46
  107.3 68.1 %all-gather.15.cloned.1.call-done = f32[64,256,128]{2,1,0:T(8,128)} async-done(((f32[2,256,128]{2,1,0:T(8,128)}), f32[64,256,128]{2,1,0:T(8,128)}) %all-gather.15.cloned.1.call-update) | async-done | bytes 8388624 | tf_op jit(solution)/shard_map/all_gather | solution.py:44
  175.4 0.0 copy-start
  175.4 8.3 %copy.83 = f32[4,8,2,256,128]{4,1,3,0,2:T(8,128)S(1)} copy(f32[4,8,2,256,128]{4,3,2,1,0:T(8,128)} %bitcast.106) | data formatting | bytes 16777216 | tf_op jit(solution)/shard_map/reshape | solution.py:46
  183.6 0.0 copy-done
  183.6 4.0 fusion.29
  187.6 3.8 fusion.28
  191.4 62.9 %all-gather.17.cloned.1.call-done = f32[64,256,128]{2,1,0:T(8,128)} async-done(((f32[2,256,128]{2,1,0:T(8,128)}), f32[64,256,128]{2,1,0:T(8,128)}) %all-gather.17.cloned.1.call-update) | async-done | bytes 8388624 | tf_op jit(solution)/shard_map/all_gather | solution.py:44
  254.4 8.5 %copy.82 = f32[4,8,2,256,128]{4,1,3,0,2:T(8,128)S(1)} copy(f32[4,8,2,256,128]{4,3,2,1,0:T(8,128)} %bitcast.105) | data formatting | bytes 16777216 | tf_op jit(solution)/shard_map/reshape | solution.py:46
  262.8 0.0 copy-start.4
  262.8 0.0 copy-start.2
  262.9 4.7 fusion.27
  267.6 0.0 copy-start.3
  267.6 0.0 copy-start.1
  267.6 0.0 copy-done.4
  267.6 2.4 fusion.18
  270.0 0.0 copy-done.2
  270.0 1.9 fusion.21
  271.9 0.0 copy-done.3
  271.9 2.4 fusion.12
  274.2 0.0 copy-done.1
  274.3 2.0 fusion.9
  276.3 0.0 copy-start.5
  276.3 4.6 fusion.24
  280.9 4.7 fusion.3
  285.7 0.0 all-gather.9.cloned.1.call-update
  285.7 0.0 all-gather.11.cloned.1.call-start
  285.7 0.0 copy-done.5
  285.7 0.5 all-gather.11.cloned.1.call-update
  286.3 75.6 %all-gather.9.cloned.1.call-done = f32[2048,1024]{1,0:T(8,128)} async-done(((f32[64,1024]{1,0:T(8,128)}), f32[2048,1024]{1,0:T(8,128)}) %all-gather.9.cloned.1.call-update) | async-done | bytes 8388624 | tf_op jit(solution)/shard_map/all_gather | solution.py:60
  361.8 1.0 dynamic-slice_bitcast_fusion.1
  362.8 0.8 copy.39
  363.6 77.6 %all-gather.11.cloned.1.call-done = f32[2048,1024]{1,0:T(8,128)} async-done(((f32[64,1024]{1,0:T(8,128)}), f32[2048,1024]{1,0:T(8,128)}) %all-gather.11.cloned.1.call-update) | async-done | bytes 8388624 | tf_op jit(solution)/shard_map/all_gather | solution.py:57
  441.3 1.0 dynamic-slice_bitcast_fusion
  442.2 0.8 copy.40
  443.1 31.4 %fusion.1 = f32[2048,1984]{0,1:T(8,128)} fusion(f32[2048,1024]{1,0:T(8,128)} %all-gather.11.cloned.1.call-done, f32[2048,1984]{0,1:T(8,128)} %param.13), kind=kOutput, calls=%fused_computation.6 | convolution fusion | flops 24964497408 | bytes 32768000 | tf_op jit(solution)/shard_map/dot_general | solution.py:10
  474.5 36.1 %bitcast_subtract_fusion = f32[1984,2048]{1,0:T(8,128)} fusion(f32[1984,2048]{1,0:T(8,128)} %param.12, f32[2048,1984]{0,1:T(8,128)} %fusion.1, f32[2048,1024]{1,0:T(8,128)} %all-gather.9.cloned.1.call-done, f32[2048,1984]{0,1:T(8,128)} %param.13), kind=kOutput, calls=%fused_computation | convolution fusion | flops 24972623872 | bytes 65273856 | tf_op jit(solution)/shard_map/dot_general | solution.py:10
  (2 shorter events, 0.1 us)
Async XLA Ops:
  7.2 88.6 %all-gather.13.cloned.1.call-start = ((), (), s32[]{:S(2)}) async-start(), calls=%async_computation.3 | async-start | bytes 8650752 | tf_op jit(solution)/shard_map/all_gather | solution.py:44
  9.9 165.5 %all-gather.15.cloned.1.call-start = ((), (), s32[]{:S(2)}) async-start(), calls=%async_computation.4 | async-start | bytes 8650752 | tf_op jit(solution)/shard_map/all_gather | solution.py:44
  12.6 241.8 %all-gather.17.cloned.1.call-start = ((), (), s32[]{:S(2)}) async-start(), calls=%async_computation.5 | async-start | bytes 8650752 | tf_op jit(solution)/shard_map/all_gather | solution.py:44
  15.3 346.5 %all-gather.9.cloned.1.call-start = ((), (), s32[]{:S(2)}) async-start(), calls=%async_computation.1 | async-start | bytes 8650752 | tf_op jit(solution)/shard_map/all_gather | solution.py:60
  175.4 8.3 %copy-start = (f32[4,8,2,256,128]{4,1,3,0,2:T(8,128)S(1)}, f32[4,8,2,256,128]{4,1,3,0,2:T(8,128)}, u32[]{:S(2)}) copy-start(f32[4,8,2,256,128]{4,1,3,0,2:T(8,128)} %copy.84) | copy-start | bytes 25165828
  262.8 4.8 copy-start.4
  262.8 7.1 %copy-start.2 = (f32[1,4,256,8,128]{4,3,2,1,0:T(8,128)S(1)}, f32[1,4,256,8,128]{4,3,2,1,0:T(8,128)}, u32[]{:S(2)}) copy-start(f32[1,4,256,8,128]{4,3,2,1,0:T(8,128)} %get-tuple-element.16) | copy-start | bytes 12582916
  267.6 4.3 copy-start.3
  267.6 6.7 %copy-start.1 = (f32[1,4,256,8,128]{4,3,2,1,0:T(8,128)S(1)}, f32[1,4,256,8,128]{4,3,2,1,0:T(8,128)}, u32[]{:S(2)}) copy-start(f32[1,4,256,8,128]{4,3,2,1,0:T(8,128)} %get-tuple-element.14) | copy-start | bytes 12582916
  276.3 9.4 %copy-start.5 = (f32[64,1024]{1,0:T(8,128)}, f32[64,1024]{1,0:T(8,128)S(1)}, u32[]{:S(2)}) copy-start(f32[64,1024]{1,0:T(8,128)S(1)} %fusion.9) | copy-start | bytes 786436
  285.7 155.6 %all-gather.11.cloned.1.call-start = ((), (), s32[]{:S(2)}) async-start(), calls=%async_computation.2 | async-start | bytes 8650752 | tf_op jit(solution)/shard_map/all_gather | solution.py:57
Sparse Core Ops, SparseCore 0:
  11.6 84.1 all-gather.12
  99.3 75.9 all-gather.14
  178.4 75.9 all-gather.16
  285.8 75.9 all-gather.8
  365.2 75.9 all-gather.10

commit v2 on v1

v2 whole, which is shorter than its diff:
```python
import jax
import jax.numpy as jnp
from jax import lax
from jax.sharding import Mesh, PartitionSpec as P

CHIPS = ("row", "z")
COL = ("z", "core")


def times(left, right, left_dim, right_dim):
    return lax.dot_general(
        left,
        right,
        (((left_dim,), (right_dim,)), ((), ())),
        precision=lax.Precision.HIGH,
        preferred_element_type=jnp.float32,
    )


def shards(
    g_first,
    g_second,
    y_head,
    l_rows,
    ut_first_inv,
    ut_cross,
    ut_second_inv,
    lt_second_inv,
    lt_cross,
    lt_first_inv,
):
    panel = l_rows.shape[0] // 2
    rows, zs, cores = (lax.axis_size(axis) for axis in ("row", "z", "core"))
    row = lax.axis_index("row")
    col = lax.axis_index("z") * cores + lax.axis_index("core")
    depth, total = g_first.shape
    width = total // rows

    def own_columns(g):
        parts = g.T.reshape(cores, rows, zs, width // (zs * cores), depth)
        parts = lax.dynamic_index_in_dim(parts, row, 1, keepdims=False)
        return parts.transpose(1, 0, 2, 3).reshape(width, depth)

    def swap_blocks(x, outer, inner):
        pieces = jnp.split(x, outer * inner, axis=-1)
        order = [a * inner + b for b in range(inner) for a in range(outer)]
        return jnp.concatenate([pieces[place] for place in order], axis=-1)

    g = jnp.stack([own_columns(g_first), own_columns(g_second)], axis=1)
    g = lax.all_to_all(g, COL, 0, 2, tiled=True)
    g = swap_blocks(g, zs, cores)

    def spread(x, chips=CHIPS):
        across = lax.all_gather(x, chips, axis=0, tiled=True)
        return lax.all_gather(across, "core", axis=0, tiled=True)

    def gather_pair(by_row, by_col):
        return spread(jnp.stack([by_row, by_col.T])[None], CHIPS[::-1])

    def arrange(blocks):
        tall, wide = blocks.shape[2:]
        blocks = blocks.reshape(cores * zs, rows, 2, tall, wide).transpose(2, 1, 3, 0, 4)
        return blocks.reshape(2, panel, panel)

    first_pair = arrange(gather_pair(ut_first_inv, ut_cross))
    second_pair = arrange(gather_pair(ut_second_inv, lt_second_inv))
    third_blocks = gather_pair(lt_cross, lt_first_inv)

    y_first = times(g[:, 0], first_pair[0], 1, 1)
    shifted = g[:, 1] - times(y_first, first_pair[1], 1, 0)
    y_second = times(shifted, second_pair[0], 1, 1)
    x_second = times(y_second, second_pair[1], 1, 0)
    x_second, third_blocks = lax.optimization_barrier((x_second, third_blocks))
    third_pair = arrange(third_blocks)
    second_all = spread(swap_blocks(x_second, cores, zs))
    corrected = y_first - times(x_second, third_pair[0], 1, 1)
    x_first = times(corrected, third_pair[1], 1, 0)
    x_first, second_all = lax.optimization_barrier((x_first, second_all))
    first_all = spread(swap_blocks(x_first, cores, zs))

    head = y_head - times(l_rows[panel:], second_all, 0, 1)
    head = head - times(l_rows[:panel], first_all, 0, 1)

    def own_block(x):
        return lax.dynamic_slice(x, (row * width, col * depth), (width, depth)).T

    return (own_block(first_all), own_block(second_all), head)


def solution(mesh):
    rows, cols = mesh.devices.shape
    split = Mesh(mesh.devices.reshape(rows, cols // 2, 2), ("row", "z", "core"))
    by_col, by_both = P(COL, None), P(("row",) + COL, None)
    return jax.shard_map(
        shards,
        mesh=split,
        in_specs=(
            by_col,
            by_col,
            by_both,
            P(None, ("row",) + COL),
            P("row", COL),
            P(COL, "row"),
            P("row", COL),
            P(COL, "row"),
            P("row", COL),
            P(COL, "row"),
        ),
        out_specs=(P(COL, "row"), P(COL, "row"), by_both),
        check_vma=False,
    )
```

time: 527 us -> 580 us (1.10)
  waiting for transfers between devices: 337 us -> 409 us
  blocking collectives: 26.5 us -> 18.4 us
  local copies, waits for them, and re-layouts: 48.8 us -> 41.5 us
    all_gather x5 -> x10, waiting for transfers between devices: 336 us -> 409 us  [the longest x5 390 us: spread(): across = lax.all_gather(x, chips, axis=0, tiled=True)]
    reshape x3 -> x0, local copies, waits for them, and re-layouts: 28.2 us -> none  [gather_pair(): blocks = blocks.reshape(rows, cols, 2, tall, wide).transpose(2, 0, 3, 1, 4)]
    all_to_all x1, blocking collectives: 26.5 us -> 18.4 us  [shards(): g = lax.all_to_all(g, COL, 0, 2, tiled=True)]
    slice x0 -> x3, local copies, waits for them, and re-layouts: none -> 7.29 us  [the longest x1 2.43 us: shards(): y_second = times(shifted, second_pair[0], 1, 1)]
    slice x1 -> x2, local copies, waits for them, and re-layouts: 3.98 us -> 10.8 us  [shards(): shifted = g[:, 1] - times(y_first, first_pair[1], 1, 0)]
  transfers between devices with their start and end apart: 5 -> 10, of which waited for: 5 -> 8; matrix products, arithmetic and copies ran while one was open for 7% -> 15% of each run, Pallas kernels for 0% -> 0%
where the time goes in v2:
time: 580 us; the launch traced here: 570 us
  waiting for transfers between devices  409 us (71%)
  matrix products  80.2 us (14%)
  local copies, waits for them, and re-layouts  41.5 us (7%)
  blocking collectives  18.4 us (3%)
  between operations  14.8 us (3%)
    all_gather x5, waiting for transfers between devices, spread(): across = lax.all_gather(x, chips, axis=0, tiled=True)  390 us
    dot_general x8, matrix products, times(): lax.dot_general(left, right, (((left_dim,), (right_dim,)), ((), ())), pre...  80.2 us
    all_gather x5, waiting for transfers between devices, spread(): return lax.all_gather(across, 'core', axis=0, tiled=True)  19.4 us
    all_to_all x1, blocking collectives, shards(): g = lax.all_to_all(g, COL, 0, 2, tiled=True)  18.4 us
  transfers between devices with their start and end apart: 10, of which 8 were waited for; matrix products, arithmetic and copies ran while one was open for 15% of the time, Pallas kernels for 0%

profile of v2, /device:TPU:0, one launch (start us, length us, event | category | flops | bytes accessed | tf_op | source)
XLA Modules:
  0.0 570.2 jit_solution(10385346080191860450)
XLA Ops:
  7.2 0.0 all-gather.28.cloned.1.call-start
  7.2 1.0 copy.51
  8.2 1.6 pad_maximum_fusion.1
  9.8 0.0 all-gather.28.cloned.1.call-update
  9.9 0.0 all-gather.30.cloned.1.call-start
  9.9 1.0 copy.54
  10.9 1.6 pad_maximum_fusion.2
  12.5 0.0 all-gather.30.cloned.1.call-update
  12.6 0.0 all-gather.32.cloned.1.call-start
  12.6 1.0 copy.57
  13.6 1.6 pad_maximum_fusion.3
  15.2 0.0 all-gather.32.cloned.1.call-update
  15.3 0.0 all-gather.14.cloned.1.call-start
  15.3 74.8 %all-gather.28.cloned.1.call-done = f32[32,256,128]{2,1,0:T(8,128)} async-done(((f32[2,256,128]{2,1,0:T(8,128)}), f32[32,256,128]{2,1,0:T(8,128)}) %all-gather.28.cloned.1.call-update) | async-done | bytes 4194320 | tf_op jit(solution)/shard_map/all_gather | solution.py:54
  90.2 0.0 all-gather.14.cloned.1.call-update
  90.2 0.0 all-gather.16.cloned.1.call-start
  90.2 78.0 %all-gather.30.cloned.1.call-done = f32[32,256,128]{2,1,0:T(8,128)} async-done(((f32[2,256,128]{2,1,0:T(8,128)}), f32[32,256,128]{2,1,0:T(8,128)}) %all-gather.30.cloned.1.call-update) | async-done | bytes 4194320 | tf_op jit(solution)/shard_map/all_gather | solution.py:54
  168.3 0.0 all-gather.18.cloned.1.call-start
  168.3 78.0 %all-gather.32.cloned.1.call-done = f32[32,256,128]{2,1,0:T(8,128)} async-done(((f32[2,256,128]{2,1,0:T(8,128)}), f32[32,256,128]{2,1,0:T(8,128)}) %all-gather.32.cloned.1.call-update) | async-done | bytes 4194320 | tf_op jit(solution)/shard_map/all_gather | solution.py:54
  246.3 0.0 all-gather.18.cloned.1.call-update
  246.3 0.0 all-gather.20.cloned.1.call-start
  246.4 0.3 copy.45
  246.7 0.3 copy.47
  247.2 0.4 copy.49
  247.6 18.4 %all_to_all.18 = f32[512,2,128]{2,1,0:T(2,128)S(1)} all-to-all(f32[512,2,128]{2,1,0:T(2,128)S(1)} %copy.49), channel_id=1, replica_groups=mesh['row'=4,'z'=4,'core'=2] {'z','core'}, dimensions={0} | all-to-all | bytes 1048576 | tf_op jit(solution)/shard_map/all_to_all | solution.py:50
  266.0 0.3 copy.97
  266.3 0.1 all_to_all.16
  266.5 0.0 all-gather.14.cloned.1.call-done
  266.6 6.3 %fusion.29 = (f32[1,4,256,8,128]{4,2,0,1,3:T(8,128)S(1)}, f32[1,4,256,8,128]{4,2,0,1,3:T(8,128)}) fusion(f32[2,4,256,8,128]{4,2,0,1,3:T(8,128)} %bitcast.113), kind=kLoop, calls=%fused_computation.62 | loop fusion | bytes 16777216 | tf_op jit(solution)/shard_map/slice | solution.py:70
  272.8 4.6 copy.53
  277.4 11.2 %all-gather.16.cloned.1.call-done = f32[32,2,256,128]{3,2,1,0:T(8,128)} async-done(((f32[16,2,256,128]{3,2,1,0:T(8,128)}), f32[32,2,256,128]{3,2,1,0:T(8,128)}) %all-gather.16.cloned.1.call-update) | async-done | bytes 8388624 | tf_op jit(solution)/shard_map/all_gather | solution.py:55
  288.6 4.0 fusion.28
  292.6 2.4 copy.56
  295.1 2.4 copy.55
  297.5 2.4 copy.52
  300.0 0.2 copy-start
  300.2 2.4 fusion.18
  302.6 0.6 copy-done
  303.1 1.9 fusion.21
  305.0 2.4 fusion.12
  307.4 1.9 fusion.9
  309.3 1.8 all-gather.18.cloned.1.call-done
  311.2 0.7 copy-done.4
  311.9 0.0 all-gather.22.cloned.1.call-start
  312.0 79.6 %all-gather.20.cloned.1.call-done = f32[1024,1024]{1,0:T(8,128)} async-done(((f32[64,1024]{1,0:T(8,128)}), f32[1024,1024]{1,0:T(8,128)}) %all-gather.20.cloned.1.call-update) | async-done | bytes 4194320 | tf_op jit(solution)/shard_map/all_gather | solution.py:54
  391.5 0.0 all-gather.22.cloned.1.call-update
  391.5 0.4 all-gather.24.cloned.1.call-start
  392.0 4.0 fusion.27
  396.0 2.4 copy.59
  398.4 2.4 copy.58
  400.9 2.4 fusion.24
  403.3 1.9 fusion.3
  405.1 6.4 %all-gather.22.cloned.1.call-done = f32[2048,1024]{1,0:T(8,128)} async-done(((f32[1024,1024]{1,0:T(8,128)}), f32[2048,1024]{1,0:T(8,128)}) %all-gather.22.cloned.1.call-update) | async-done | bytes 8388624 | tf_op jit(solution)/shard_map/all_gather | solution.py:55
  411.7 0.7 copy-done.5
  412.3 0.0 all-gather.24.cloned.1.call-update
  412.4 0.2 all-gather.26.cloned.1.call-start
  412.6 79.4 %all-gather.24.cloned.1.call-done = f32[1024,1024]{1,0:T(8,128)} async-done(((f32[64,1024]{1,0:T(8,128)}), f32[1024,1024]{1,0:T(8,128)}) %all-gather.24.cloned.1.call-update) | async-done | bytes 4194320 | tf_op jit(solution)/shard_map/all_gather | solution.py:54
  492.0 0.0 all-gather.26.cloned.1.call-update
  492.0 1.0 dynamic-slice_bitcast_fusion
  493.0 0.8 copy.61
  493.8 31.4 %fusion.1 = f32[2048,1984]{0,1:T(8,128)} fusion(f32[2048,1024]{1,0:T(8,128)} %all-gather.22.cloned.1.call-done, f32[2048,1984]{0,1:T(8,128)} %param.13), kind=kOutput, calls=%fused_computation.3 | convolution fusion | flops 24964497408 | bytes 32768000 | tf_op jit(solution)/shard_map/dot_general | solution.py:11
  525.2 1.0 dynamic-slice_bitcast_fusion.1
  526.2 0.8 copy.60
  527.0 36.1 %bitcast_subtract_fusion = f32[1984,2048]{1,0:T(8,128)} fusion(f32[1984,2048]{1,0:T(8,128)} %param.12, f32[2048,1984]{0,1:T(8,128)} %fusion.1, f32[2048,1024]{1,0:T(8,128)} %all-gather.26.cloned.1.call-done, f32[2048,1984]{0,1:T(8,128)} %param.13), kind=kOutput, calls=%fused_computation | convolution fusion | flops 24972623872 | bytes 65273856 | tf_op jit(solution)/shard_map/dot_general | solution.py:11
  (39 shorter events, 0.4 us)
Async XLA Ops:
  7.2 83.0 %all-gather.28.cloned.1.call-start = ((), (), s32[]{:S(2)}) async-start(), calls=%async_computation.8 | async-start | bytes 4456448 | tf_op jit(solution)/shard_map/all_gather | solution.py:54
  9.9 158.4 %all-gather.30.cloned.1.call-start = ((), (), s32[]{:S(2)}) async-start(), calls=%async_computation.9 | async-start | bytes 4456448 | tf_op jit(solution)/shard_map/all_gather | solution.py:54
  12.6 233.7 %all-gather.32.cloned.1.call-start = ((), (), s32[]{:S(2)}) async-start(), calls=%async_computation.10 | async-start | bytes 4456448 | tf_op jit(solution)/shard_map/all_gather | solution.py:54
  15.3 251.3 %all-gather.14.cloned.1.call-start = ((), (), s32[]{:S(2)}) async-start(), calls=%async_computation.1 | async-start | bytes 12582912 | tf_op jit(solution)/shard_map/all_gather | solution.py:55
  90.2 198.4 %all-gather.16.cloned.1.call-start = ((), (), s32[]{:S(2)}) async-start(), calls=%async_computation.2 | async-start | bytes 12582912 | tf_op jit(solution)/shard_map/all_gather | solution.py:55
  168.2 78.1 %copy-start.2 = (f32[128,2048]{1,0:T(8,128)S(1)}, f32[128,2048]{1,0:T(8,128)}, u32[]{:S(2)}) copy-start(f32[128,2048]{1,0:T(8,128)} %param.10) | copy-start | bytes 3145732
  168.2 78.5 %copy-start.3 = (f32[128,2048]{1,0:T(8,128)S(1)}, f32[128,2048]{1,0:T(8,128)}, u32[]{:S(2)}) copy-start(f32[128,2048]{1,0:T(8,128)} %param.11) | copy-start | bytes 3145732
  168.3 142.8 %all-gather.18.cloned.1.call-start = ((), (), s32[]{:S(2)}) async-start(), calls=%async_computation.3 | async-start | bytes 12582912 | tf_op jit(solution)/shard_map/all_gather | solution.py:55
  246.3 145.2 %all-gather.20.cloned.1.call-start = ((), (), s32[]{:S(2)}) async-start(), calls=%async_computation.4 | async-start | bytes 4456448 | tf_op jit(solution)/shard_map/all_gather | solution.py:54
  295.1 2.5 copy-start.1
  300.0 3.2 copy-start
  311.2 0.7 copy-start.4
  311.9 99.6 %all-gather.22.cloned.1.call-start = ((), (), s32[]{:S(2)}) async-start(), calls=%async_computation.5 | async-start | bytes 12582912 | tf_op jit(solution)/shard_map/all_gather | solution.py:55
  391.5 100.4 %all-gather.24.cloned.1.call-start = ((), (), s32[]{:S(2)}) async-start(), calls=%async_computation.6 | async-start | bytes 4456448 | tf_op jit(solution)/shard_map/all_gather | solution.py:54
  411.6 0.7 copy-start.5
  412.4 112.9 %all-gather.26.cloned.1.call-start = ((), (), s32[]{:S(2)}) async-start(), calls=%async_computation.7 | async-start | bytes 12582912 | tf_op jit(solution)/shard_map/all_gather | solution.py:55
Sparse Core Ops, SparseCore 0:
  11.3 78.7 all-gather.27
  93.5 74.6 all-gather.29
  171.6 74.6 all-gather.31
  247.7 18.4 all-gather.13
  267.6 21.0 all-gather.15
  290.0 21.0 all-gather.17
  314.4 77.0 all-gather.19
  393.0 18.4 all-gather.21
  414.9 77.0 all-gather.23
  493.4 18.4 all-gather.25
